TPU v7x, 256 devices: a whole 4x4x8 slice. The times are simulated.
256 devices in a mesh: ma: 32 (over z, y), freq: 8 (over x, core).
Axes of the slice: x: 4, y: 4, z: 8, core: 2. Of those that a mesh axis runs over, the one named last changes fastest.
Arguments:
- visibilities: bfloat16 [512, 32, 4, 512], P('ma', 'freq'), may hold values from -6 to 6
- transfer: bfloat16 [32, 64, 512, 1024], P('freq', 'ma'), may hold values from -1 to 1, as said below
- noise_weight: float32 [32, 512], P('freq'), may hold values from 1 to 12, as said below
- freq_prior: float32 [32, 32], P('freq'), may hold values from -1 to 5, as said below
Outputs:
- sky_map: float32 [32, 64, 4, 1024], P('freq', 'ma')
- residual: float32 [32, 64, 4, 1024], P('freq', 'ma')
- direction: float32 [32, 64, 4, 1024], P('freq', 'ma')
Inputs may be any that keep to these rules, and one draw needn't show every extreme that they name: Real transfer blocks of the m-modes in the window. `noise_weight`: positive weights. `freq_prior`: symmetric positive definite.
All inputs are finite; a program needn't handle non-finite values.
Results may differ from a plain program's by a relative error of at most 0.0056.
Values may be sent and summed in bfloat16 or wider, within the bound.
A program may use at most 64 MiB of HBM per device.

v0:
```python
import math
import jax
import jax.numpy as jnp
from jax import lax
from jax.sharding import PartitionSpec as P


def harmonic_lookup(harmonic_number, leading_epoch, epoch_number, whole_epoch_grid):
    harmonic_slot = jnp.arange(harmonic_number, dtype=jnp.int32)
    observing_epochs = leading_epoch + jnp.arange(epoch_number, dtype=jnp.int32)
    rotation_argument = harmonic_slot[:, None] * observing_epochs[None, :] % whole_epoch_grid
    rotation_radians = rotation_argument.astype(jnp.float32) * (2.0 * math.pi / whole_epoch_grid)
    return (
        (jnp.cos(rotation_radians) + jnp.sin(rotation_radians))
        * (1.0 / math.sqrt(whole_epoch_grid))
    ).astype(jnp.bfloat16)


def local(visibilities, transfer, noise_weight, freq_prior):
    epochs_each_shard, frequency_per_device, realization_count, baseline_pairs = visibilities.shape
    harmonics_each_shard = transfer.shape[1]
    harmonic_amount = lax.axis_size("ma")
    whole_epoch_grid = epochs_each_shard * harmonic_amount
    column_total = frequency_per_device * realization_count * baseline_pairs
    flat_vis = visibilities.reshape(epochs_each_shard, column_total)
    leading_epoch = lax.axis_index("ma") * epochs_each_shard
    cas_rows = harmonic_lookup(
        harmonics_each_shard * lax.axis_size("ma"),
        leading_epoch,
        epochs_each_shard,
        whole_epoch_grid,
    )
    mode_totals = lax.psum_scatter(
        jnp.dot(cas_rows, flat_vis, preferred_element_type=jnp.float32),
        "ma",
        scatter_dimension=0,
        tiled=True,
    )
    visibility_modes = mode_totals.reshape(
        harmonics_each_shard, frequency_per_device, realization_count, baseline_pairs
    )
    weighted = (noise_weight[None, :, None, :] * visibility_modes).astype(jnp.bfloat16)
    right_side = jnp.einsum(
        "fmbs,mfkb->fmks", transfer, weighted, preferred_element_type=jnp.float32
    )
    right_low = right_side.astype(jnp.bfloat16)
    observed = jnp.einsum(
        "fmbs,fmks->fmkb", transfer, right_low, preferred_element_type=jnp.float32
    )
    scaled = (noise_weight[:, None, None, :] * observed).astype(jnp.bfloat16)
    adjoint = jnp.einsum("fmbs,fmkb->fmks", transfer, scaled, preferred_element_type=jnp.float32)
    coupled = jnp.einsum(
        "fg,gmks->fmks",
        freq_prior,
        lax.all_gather(right_side, "freq", axis=0, tiled=True),
        precision=lax.Precision.HIGHEST,
    )
    applied = adjoint + coupled
    local_norm = jnp.sum(right_side * right_side, axis=(0, 1, 3))
    local_curve = jnp.sum(right_side * applied, axis=(0, 1, 3))
    norm_now = lax.psum(local_norm, ("ma", "freq"))
    curvature = lax.psum(local_curve, ("ma", "freq"))
    step_plain = norm_now / curvature
    residual = right_side - step_plain[None, None, :, None] * applied
    norm_next = lax.psum(jnp.sum(residual * residual, axis=(0, 1, 3)), ("ma", "freq"))
    sky_map = step_plain[None, None, :, None] * right_side
    direction = residual + (norm_next / norm_now)[None, None, :, None] * right_side
    return (sky_map, residual, direction)


def solution(mesh):
    return jax.shard_map(
        local,
        mesh=mesh,
        in_specs=(
            P("ma", "freq", None, None),
            P("freq", "ma", None, None),
            P("freq", None),
            P("freq", None),
        ),
        out_specs=(
            P("freq", "ma", None, None),
            P("freq", "ma", None, None),
            P("freq", "ma", None, None),
        ),
        check_vma=False,
    )
```

profile of v0, /device:TPU:1, one launch (start us, length us, event | category | flops | bytes accessed | tf_op | source)
XLA Modules:
  0.0 370.0 jit_solution(2050857011195431761)
XLA Ops:
  7.2 0.0 copy-start
  7.2 0.0 copy-start.2
  7.2 0.0 all-reduce.4.cloned.1.call-start
  7.2 1.1 reshape.20
  8.4 1.9 fusion.16
  10.3 0.0 all-reduce.4.cloned.1.call-update
  10.3 0.0 all-gather.2.cloned.1.call-start
  10.3 1.3 dynamic-slice
  12.3 153.0 %all-reduce.4.cloned.1.call-done = f32[64,8192]{1,0:T(8,128)} async-done(((f32[64,8192]{1,0:T(8,128)}), f32[64,8192]{1,0:T(8,128)}) %all-reduce.4.cloned.1.call-update) | async-done | bytes 2097168
  165.3 1.0 constant_dynamic-slice_fusion
  166.3 0.1 reshape.21
  166.3 5.3 %fusion.6 = f32[4,2,4,1024]{3,2,1,0:T(4,128)} fusion(bf16[4,2,512,1024]{3,2,1,0:T(8,128)(2,1)} %param.5, f32[2,4,4,512]{3,2,1,0:T(4,128)S(1)} %reshape.21, f32[4,512]{1,0:T(4,128)} %param.6), kind=kOutput, calls=%fused_computation.14 | convolution fusion | flops 33587200 | bytes 8593408 | tf_op jit(solution)/shard_map/fmbs,mfkb->fmks/dot_general | solution.py:43
  171.6 0.0 all-gather.2.cloned.1.call-update
  171.6 27.8 %all-gather.2.cloned.1.call-done = f32[32,2,4,1024]{3,2,1,0:T(4,128)} async-done(((f32[4,2,4,1024]{3,2,1,0:T(4,128)}), f32[32,2,4,1024]{3,2,1,0:T(4,128)}) %all-gather.2.cloned.1.call-update) | async-done | bytes 1048592 | tf_op jit(solution)/shard_map/all_gather | solution.py:55
  199.4 0.0 copy-done
  199.4 2.4 fusion.1
  201.8 0.0 copy-done.2
  201.8 0.0 copy-start.1
  201.8 9.3 %multiply_reduce_fusion.1 = (f32[4]{0:T(128)S(1)}, f32[4]{0:T(128)S(1)}, f32[4,2,4,1024]{3,2,1,0:T(4,128)S(1)}) fusion(f32[4,2,4,1024]{3,2,1,0:T(4,128)} %fusion.6, f32[2,4,1024,4]{2,3,1,0:T(4,128)S(1)} %fusion.1, bf16[4,2,512,1024]{3,2,1,0:T(8,128)(2,1)} %param.5, f32[4,512]{1,0:T(4,128)S(1)} %copy-done.2), kind=kOutput, calls=%fused_computation.8 | convolution fusion | flops 67338240 | bytes 8790048 | tf_op jit(solution)/shard_map/fmbs,fmkb->fmks/dot_general | solution.py:51
  211.2 76.0 %all-reduce.1 = (f32[4]{0:T(128)S(1)}, f32[4]{0:T(128)S(1)}) all-reduce(f32[4]{0:T(128)S(1)} %get-tuple-element.4, f32[4]{0:T(128)S(1)} %get-tuple-element.3), channel_id=1, replica_groups=mesh['ma'=32,'freq'=8] {'ma','freq'}, use_global_device_ids=true, to_apply=%region_2.3 | all-reduce | flops 8 | bytes 64 | tf_op jit(solution)/shard_map/psum | solution.py:61
  287.2 0.0 copy-done.1
  287.2 0.9 multiply_reduce_fusion
  288.1 0.0 copy-start.3
  288.1 74.3 %psum.23 = f32[4]{0:T(128)S(1)} all-reduce(f32[4]{0:T(128)S(1)} %get-tuple-element.7), channel_id=1, replica_groups=mesh['ma'=32,'freq'=8] {'ma','freq'}, use_global_device_ids=true, to_apply=%region_6.7 | all-reduce | flops 4 | bytes 32 | tf_op jit(solution)/shard_map/psum | solution.py:65
  362.4 0.8 multiply_add_fusion
  363.1 0.0 copy-done.3
  (3 shorter events, 0.0 us)
Async XLA Ops:
  7.2 192.2 %copy-start = (f32[4,32]{1,0:T(4,128)S(1)}, f32[4,32]{1,0:T(4,128)}, u32[]{:S(2)}) copy-start(f32[4,32]{1,0:T(4,128)} %param.7) | copy-start | bytes 1540
  7.2 194.6 %copy-start.2 = (f32[4,512]{1,0:T(4,128)S(1)}, f32[4,512]{1,0:T(4,128)}, u32[]{:S(2)}) copy-start(f32[4,512]{1,0:T(4,128)} %param.6) | copy-start | bytes 24580
  7.2 158.1 %all-reduce.4.cloned.1.call-start = ((), (), s32[]{:S(2)}) async-start(), calls=%async_computation.1 | async-start | bytes 4194304
  10.3 189.1 %all-gather.2.cloned.1.call-start = ((), (), s32[]{:S(2)}) async-start(), calls=%async_computation | async-start | bytes 1179648 | tf_op jit(solution)/shard_map/all_gather | solution.py:55
  201.8 85.4 %copy-start.1 = (f32[4,2,4,1024]{3,2,1,0:T(4,128)S(1)}, f32[4,2,4,1024]{3,2,1,0:T(4,128)}, u32[]{:S(2)}) copy-start(f32[4,2,4,1024]{3,2,1,0:T(4,128)} %fusion.6) | copy-start | bytes 393220
  288.1 75.0 %copy-start.3 = (f32[4,2,4,1024]{3,2,1,0:T(4,128)}, f32[4,2,4,1024]{3,2,1,0:T(4,128)S(1)}, u32[]{:S(2)}) copy-start(f32[4,2,4,1024]{3,2,1,0:T(4,128)S(1)} %get-tuple-element.8) | copy-start | bytes 393220
Sparse Core Ops, SparseCore 0:
  11.5 153.6 all-reduce.3
  171.7 27.6 all-gather.1
where the time goes:
time: 370 us
  waiting for transfers between devices  181 us (49%)
  blocking collectives  150 us (41%)
  matrix products  18.9 us (5%)
  between operations  14.8 us (4%)
    unnamed x3, waiting for transfers between devices  153 us
    psum x1, blocking collectives, local(): norm_now = lax.psum(local_norm, ('ma', 'freq'))  76 us
    psum x1, blocking collectives, local(): lax.psum(jnp.sum(residual * residual, axis=(0, 1, 3)), ('ma', 'freq'))  74.3 us
    all_gather x1, waiting for transfers between devices, local(): lax.all_gather(right_side, 'freq', axis=0, tiled=True)  27.8 us
    dot_general x1, matrix products, local(): jnp.einsum('fmbs,fmkb->fmks', transfer, scaled, preferred_element_type=jn...  9.35 us
  transfers between devices with their start and end apart: 2, of which 2 were waited for; matrix products, arithmetic and copies ran while one was open for 0% of the time, Pallas kernels for 0%

commit v1 on v0

--- a/solution.py
+++ b/solution.py
@@ -62,7 +62,9 @@
     curvature = lax.psum(local_curve, ("ma", "freq"))
     step_plain = norm_now / curvature
     residual = right_side - step_plain[None, None, :, None] * applied
-    norm_next = lax.psum(jnp.sum(residual * residual, axis=(0, 1, 3)), ("ma", "freq"))
+    norm_next = jnp.sum(residual * residual, axis=(0, 1, 3))
+    for over in ("ma", "freq"):
+        norm_next = lax.psum(norm_next, over)
     sky_map = step_plain[None, None, :, None] * right_side
     direction = residual + (norm_next / norm_now)[None, None, :, None] * right_side
     return (sky_map, residual, direction)

time: 370 us -> 382 us (1.032)
  blocking collectives: 150 us -> 162 us
    psum x1 -> x2, blocking collectives: 74.3 us -> 85.8 us  [local(): norm_next = lax.psum(norm_next, over)]
where the time goes in v1:
time: 382 us
  waiting for transfers between devices  181 us (47%)
  blocking collectives  162 us (42%)
  matrix products  18.9 us (5%)
  between operations  14.8 us (4%)
    unnamed x3, waiting for transfers between devices  153 us
    psum x2, blocking collectives, local(): norm_next = lax.psum(norm_next, over)  85.8 us
    psum x1, blocking collectives, local(): norm_now = lax.psum(local_norm, ('ma', 'freq'))  76 us
    all_gather x1, waiting for transfers between devices, local(): lax.all_gather(right_side, 'freq', axis=0, tiled=True)  27.8 us
    dot_general x1, matrix products, local(): jnp.einsum('fmbs,fmkb->fmks', transfer, scaled, preferred_element_type=jn...  9.37 us
  transfers between devices with their start and end apart: 2, of which 2 were waited for; matrix products, arithmetic and copies ran while one was open for 0% of the time, Pallas kernels for 0%

profile of v1, /device:TPU:1, one launch (start us, length us, event | category | flops | bytes accessed | tf_op | source)
XLA Modules:
  0.0 381.5 jit_solution(15595548547362911668)
XLA Ops:
  7.2 0.0 copy-start
  7.2 0.0 copy-start.2
  7.2 0.0 all-reduce.4.cloned.1.call-start
  7.2 1.1 reshape.20
  8.4 1.9 fusion.16
  10.3 0.0 all-reduce.4.cloned.1.call-update
  10.3 0.0 all-gather.2.cloned.1.call-start
  10.3 1.3 dynamic-slice
  12.3 153.0 %all-reduce.4.cloned.1.call-done = f32[64,8192]{1,0:T(8,128)} async-done(((f32[64,8192]{1,0:T(8,128)}), f32[64,8192]{1,0:T(8,128)}) %all-reduce.4.cloned.1.call-update) | async-done | bytes 2097168
  165.3 1.0 constant_dynamic-slice_fusion
  166.3 0.1 reshape.21
  166.3 5.3 %fusion.6 = f32[4,2,4,1024]{3,2,1,0:T(4,128)} fusion(bf16[4,2,512,1024]{3,2,1,0:T(8,128)(2,1)} %param.5, f32[2,4,4,512]{3,2,1,0:T(4,128)S(1)} %reshape.21, f32[4,512]{1,0:T(4,128)} %param.6), kind=kOutput, calls=%fused_computation.14 | convolution fusion | flops 33587200 | bytes 8593408 | tf_op jit(solution)/shard_map/fmbs,mfkb->fmks/dot_general | solution.py:43
  171.6 0.0 all-gather.2.cloned.1.call-update
  171.6 27.8 %all-gather.2.cloned.1.call-done = f32[32,2,4,1024]{3,2,1,0:T(4,128)} async-done(((f32[4,2,4,1024]{3,2,1,0:T(4,128)}), f32[32,2,4,1024]{3,2,1,0:T(4,128)}) %all-gather.2.cloned.1.call-update) | async-done | bytes 1048592 | tf_op jit(solution)/shard_map/all_gather | solution.py:55
  199.4 0.0 copy-done
  199.4 2.4 fusion.1
  201.8 0.0 copy-done.2
  201.8 0.0 copy-start.1
  201.8 9.4 %multiply_reduce_fusion.1 = (f32[4]{0:T(128)S(1)}, f32[4]{0:T(128)S(1)}, f32[4,2,4,1024]{3,2,1,0:T(4,128)S(1)}) fusion(f32[4,2,4,1024]{3,2,1,0:T(4,128)} %fusion.6, f32[2,4,1024,4]{2,3,1,0:T(4,128)S(1)} %fusion.1, bf16[4,2,512,1024]{3,2,1,0:T(8,128)(2,1)} %param.5, f32[4,512]{1,0:T(4,128)S(1)} %copy-done.2), kind=kOutput, calls=%fused_computation.8 | convolution fusion | flops 67338240 | bytes 8790048 | tf_op jit(solution)/shard_map/fmbs,fmkb->fmks/dot_general | solution.py:51
  211.2 76.0 %all-reduce.1 = (f32[4]{0:T(128)S(1)}, f32[4]{0:T(128)S(1)}) all-reduce(f32[4]{0:T(128)S(1)} %get-tuple-element.4, f32[4]{0:T(128)S(1)} %get-tuple-element.3), channel_id=1, replica_groups=mesh['ma'=32,'freq'=8] {'ma','freq'}, use_global_device_ids=true, to_apply=%region_2.3 | all-reduce | flops 8 | bytes 64 | tf_op jit(solution)/shard_map/psum | solution.py:61
  287.2 0.0 copy-done.1
  287.2 0.9 multiply_reduce_fusion
  288.1 0.0 copy-start.3
  288.1 59.2 %psum.30 = f32[4]{0:T(128)S(1)} all-reduce(f32[4]{0:T(128)S(1)} %get-tuple-element.7), channel_id=1, replica_groups=mesh['ma'=32,'freq'=8] {'ma'}, use_global_device_ids=true, to_apply=%region_6.7 | all-reduce | flops 4 | bytes 32 | tf_op jit(solution)/shard_map/psum | solution.py:67
  347.3 26.6 %psum.31 = f32[4]{0:T(128)S(1)} all-reduce(f32[4]{0:T(128)S(1)} %psum.30), channel_id=1, replica_groups=mesh['ma'=32,'freq'=8] {'freq'}, use_global_device_ids=true, to_apply=%region_7.8 | all-reduce | flops 4 | bytes 32 | tf_op jit(solution)/shard_map/psum | solution.py:67
  373.9 0.8 multiply_add_fusion
  374.7 0.0 copy-done.3
  (3 shorter events, 0.0 us)
Async XLA Ops:
  7.2 192.2 %copy-start = (f32[4,32]{1,0:T(4,128)S(1)}, f32[4,32]{1,0:T(4,128)}, u32[]{:S(2)}) copy-start(f32[4,32]{1,0:T(4,128)} %param.7) | copy-start | bytes 1540
  7.2 194.6 %copy-start.2 = (f32[4,512]{1,0:T(4,128)S(1)}, f32[4,512]{1,0:T(4,128)}, u32[]{:S(2)}) copy-start(f32[4,512]{1,0:T(4,128)} %param.6) | copy-start | bytes 24580
  7.2 158.1 %all-reduce.4.cloned.1.call-start = ((), (), s32[]{:S(2)}) async-start(), calls=%async_computation.1 | async-start | bytes 4194304
  10.3 189.1 %all-gather.2.cloned.1.call-start = ((), (), s32[]{:S(2)}) async-start(), calls=%async_computation | async-start | bytes 1179648 | tf_op jit(solution)/shard_map/all_gather | solution.py:55
  201.8 85.4 %copy-start.1 = (f32[4,2,4,1024]{3,2,1,0:T(4,128)S(1)}, f32[4,2,4,1024]{3,2,1,0:T(4,128)}, u32[]{:S(2)}) copy-start(f32[4,2,4,1024]{3,2,1,0:T(4,128)} %fusion.6) | copy-start | bytes 393220
  288.1 86.6 %copy-start.3 = (f32[4,2,4,1024]{3,2,1,0:T(4,128)}, f32[4,2,4,1024]{3,2,1,0:T(4,128)S(1)}, u32[]{:S(2)}) copy-start(f32[4,2,4,1024]{3,2,1,0:T(4,128)S(1)} %get-tuple-element.8) | copy-start | bytes 393220
Sparse Core Ops, SparseCore 0:
  11.5 153.6 all-reduce.3
  171.7 27.6 all-gather.1
